TPU v7x, 32 devices: a whole 2x2x4 slice. The times are simulated.
32 devices in a mesh: occ: 4 (over y, core), vir: 8 (over z, x).
Axes of the slice: x: 2, y: 2, z: 4, core: 2. Of those that a mesh axis runs over, the one named last changes fastest.
Arguments:
- amplitudes: bfloat16 [8, 1024, 1024], P('occ', 'vir'), may hold values from -6 to 6
- factors: bfloat16 [24, 1024, 1024], P('vir'), may hold values from -0.0625 to 0.0625
- occ_energy: float32 [100], replicated, may hold values from -2 to -0.3
- vir_energy: float32 [1024], replicated, may hold values from 0.3 to 4
- occ_irrep: int32 [100], replicated, may hold values from 0 to 7
- vir_irrep: int32 [1024], replicated, may hold values from 0 to 7
- pair_orbitals: int32 [8, 2], replicated, may hold values from 0 to 99, as said below
Outputs:
- update: float32 [8, 1024, 1024], P('occ', 'vir')
Inputs may be any that keep to these rules, and one draw needn't show every extreme that they name: `pair_orbitals`: pair p + 4 is pair p with i and j swapped; the orbitals named by the first 4 pairs are all distinct.
All inputs are finite; a program needn't handle non-finite values.
Results may differ from a plain program's by a relative error of at most 0.0029.
Values may be sent and summed in bfloat16 or wider, within the bound.
No kernel may reach another device: no remote copies, remote signals or barrier semaphores. Data moves between devices by JAX's collectives and lax.ppermute only.
A program may use at most 128 MiB of HBM per device.

v0:
```python
import jax
import jax.numpy as jnp
from jax import lax
from jax.sharding import PartitionSpec as P


def passed_along(block, axis, distance):
    devices = range(lax.axis_size(axis))
    route = [((i - distance) % len(devices), i) for i in devices]
    return lax.ppermute(block, axis, route)


def per_device(amplitudes, factors, occ_energy, vir_energy, occ_irrep, vir_irrep, pair_orbitals):
    local_pairs = amplitudes.shape[0]
    row_count = amplitudes.shape[1]
    occ_total = occ_energy.shape[0]
    occ_devices = lax.axis_size("occ")
    gathered = lax.all_gather(amplitudes, "vir", axis=1, tiled=True)

    def half_product(factor):
        product = jnp.einsum("pcd,bd->pbc", gathered, factor, preferred_element_type=jnp.float32)
        return product.astype(jnp.bfloat16)

    halves = lax.map(half_product, factors)
    scattered = lax.psum_scatter(
        jnp.einsum("qac,qpbc->apb", factors, halves, preferred_element_type=jnp.float32),
        "vir",
        scatter_dimension=0,
        tiled=True,
    )
    own_part = jnp.transpose(scattered, (1, 0, 2))
    shifted = passed_along(own_part, "occ", occ_devices // 2)
    turned = lax.all_to_all(shifted, "vir", split_axis=2, concat_axis=1, tiled=True)
    partner = jnp.transpose(turned, (0, 2, 1))
    occ_index = lax.axis_index("occ")
    vir_index = lax.axis_index("vir")
    pair_ids = lax.dynamic_slice_in_dim(pair_orbitals, occ_index * local_pairs, local_pairs, 0)
    row_start = vir_index * row_count
    energy_rows = lax.dynamic_slice_in_dim(vir_energy, row_start, row_count, 0)
    irrep_rows = lax.dynamic_slice_in_dim(vir_irrep, row_start, row_count, 0)
    positions = jnp.arange(occ_total, dtype=jnp.int32)
    first_hot = positions[None, :] == pair_ids[:, 0:1]
    second_hot = positions[None, :] == pair_ids[:, 1:2]
    pair_energy = jnp.sum(jnp.where(first_hot, occ_energy[None, :], 0.0), axis=1) + jnp.sum(
        jnp.where(second_hot, occ_energy[None, :], 0.0), axis=1
    )
    first_irrep = jnp.sum(jnp.where(first_hot, occ_irrep[None, :], 0), axis=1)
    second_irrep = jnp.sum(jnp.where(second_hot, occ_irrep[None, :], 0), axis=1)
    pair_sym = jnp.bitwise_xor(first_irrep, second_irrep)
    combined = jnp.bitwise_xor(
        jnp.bitwise_xor(pair_sym[:, None, None], irrep_rows[None, :, None]),
        vir_irrep[None, None, :],
    )
    allowed = combined == 0
    denominator = (
        energy_rows[None, :, None] + vir_energy[None, None, :] - pair_energy[:, None, None]
    )
    return jnp.where(allowed, (own_part + partner) / denominator, jnp.float32(0.0))


def solution(mesh):
    return jax.shard_map(
        per_device,
        mesh=mesh,
        in_specs=(P("occ", "vir", None), P("vir", None, None), P(), P(), P(), P(), P()),
        out_specs=P("occ", "vir", None),
        check_vma=False,
    )
```

profile of v0, /device:TPU:0, one launch (start us, length us, event | category | flops | bytes accessed | tf_op | source)
XLA Modules:
  0.0 347.3 jit_solution(9839581713695159661)
XLA Ops:
  6.5 0.0 copy-start
  6.5 0.0 all-gather.2.cloned.1.call-start
  6.5 0.7 all-gather.2.cloned.1.call-update
  7.3 0.0 reduce-scatter.2.cloned.1.call-start
  7.3 78.3 %all-gather.2.cloned.1.call-done = bf16[2,1024,1024]{2,1,0:T(8,128)(2,1)} async-done(((bf16[2,128,1024]{2,1,0:T(8,128)(2,1)}), bf16[2,1024,1024]{2,1,0:T(8,128)(2,1)}) %all-gather.2.cloned.1.call-update) | async-done | bytes 4194320 | tf_op jit(solution)/shard_map/all_gather | solution.py:18
  85.6 27.9 %while.10 = (s32[]{:T(128)}, bf16[3,2,1024,1024]{3,2,1,0:T(8,128)(2,1)}, bf16[3,1024,1024]{2,1,0:T(8,128)(2,1)}, bf16[2,1024,1024]{2,1,0:T(8,128)(2,1)}, s32[]{:T(128)}) while((s32[]{:T(128)}, bf16[3,2,1024,1024]{3,2,1,0:T(8,128)(2,1)}, bf16[3,1024,1024]{2,1,0:T(8,128)(2,1)}, bf16[2,1024,1024]{2,1,0:T(8,128)(2,1)}, s32[]{:T(128)}) %tuple.21), condition=%wide.region_3.4_spmd, body=%wide.region_2.3_spmd.sunk | while | flops 4297064448 | bytes 10486853 | solution.py:24
  85.6 9.3 %bitcast_dynamic-update-slice_fusion.2 = bf16[3,2,1024,1024]{3,2,1,0:T(8,128)(2,1)} fusion(bf16[3,2,1024,1024]{3,2,1,0:T(8,128)(2,1)} %get-tuple-element.73, s32[]{:T(128)S(6)} %copy.22, bf16[2,1024,1024]{2,1,0:T(8,128)(2,1)} %get-tuple-element.80, bf16[3,1024,1024]{2,1,0:T(8,128)(2,1)} %get-tuple-element.79), kind=kOutput, calls=%fused_computation.clone.1 | convolution fusion | flops 4297064448 | bytes 10486784 | tf_op jit(solution)/shard_map/while/body/eval_jaxpr/pcd,bd->pbc/dot_general | solution.py:21
  95.0 9.3 %bitcast_dynamic-update-slice_fusion.2 = bf16[3,2,1024,1024]{3,2,1,0:T(8,128)(2,1)} fusion(bf16[3,2,1024,1024]{3,2,1,0:T(8,128)(2,1)} %get-tuple-element.73, s32[]{:T(128)S(6)} %copy.22, bf16[2,1024,1024]{2,1,0:T(8,128)(2,1)} %get-tuple-element.80, bf16[3,1024,1024]{2,1,0:T(8,128)(2,1)} %get-tuple-element.79), kind=kOutput, calls=%fused_computation.clone.1 | convolution fusion | flops 4297064448 | bytes 10486784 | tf_op jit(solution)/shard_map/while/body/eval_jaxpr/pcd,bd->pbc/dot_general | solution.py:21
  104.3 9.3 %bitcast_dynamic-update-slice_fusion.2 = bf16[3,2,1024,1024]{3,2,1,0:T(8,128)(2,1)} fusion(bf16[3,2,1024,1024]{3,2,1,0:T(8,128)(2,1)} %get-tuple-element.73, s32[]{:T(128)S(6)} %copy.22, bf16[2,1024,1024]{2,1,0:T(8,128)(2,1)} %get-tuple-element.80, bf16[3,1024,1024]{2,1,0:T(8,128)(2,1)} %get-tuple-element.79), kind=kOutput, calls=%fused_computation.clone.1 | convolution fusion | flops 4297064448 | bytes 10486784 | tf_op jit(solution)/shard_map/while/body/eval_jaxpr/pcd,bd->pbc/dot_general | solution.py:21
  113.6 19.4 %fusion.5 = f32[1024,2,1024]{0,2,1:T(8,128)} fusion(bf16[3,2,1024,1024]{3,2,1,0:T(8,128)(2,1)} %get-tuple-element.27, bf16[3,1024,1024]{2,1,0:T(8,128)(2,1)} %get-tuple-element.92), kind=kOutput, calls=%fused_computation.6 | convolution fusion | flops 12884901888 | bytes 27262976 | tf_op jit(solution)/shard_map/qac,qpbc->apb/dot_general | solution.py:26
  133.0 0.0 copy-start.4
  133.0 0.0 reduce-scatter.2.cloned.1.call-update
  133.0 147.8 %reduce-scatter.2.cloned.1.call-done = f32[128,2,1024]{0,2,1:T(8,128)} async-done(((f32[1024,2,1024]{0,2,1:T(8,128)}), f32[128,2,1024]{0,2,1:T(8,128)}) %reduce-scatter.2.cloned.1.call-update) | async-done | bytes 1048592 | tf_op jit(solution)/shard_map/reduce_scatter | solution.py:25
  280.9 1.5 collective-permute-start
  282.3 23.7 %collective-permute-done = f32[2,128,1024]{1,2,0:T(8,128)S(1)} collective-permute-done((f32[2,128,1024]{1,2,0:T(8,128)}, f32[2,128,1024]{1,2,0:T(8,128)S(1)}, u32[]{:S(2)}, u32[]{:S(2)}) %collective-permute-start) | collective-permute-done | bytes 1048608 | tf_op jit(solution)/shard_map/ppermute | solution.py:10
  306.0 1.8 copy.15
  307.8 3.8 %all-to-all-start = ((f32[2,128,1024]{1,0,2:T(2,128)}), f32[2,128,1024]{1,0,2:T(2,128)S(1)}, u32[]{:S(2)}, u32[]{:S(2)}) async-start(f32[2,128,1024]{1,0,2:T(2,128)} %copy.15), calls=%async_computation.1 | async-start | bytes 2097152 | tf_op jit(solution)/shard_map/all_to_all | solution.py:33
  311.6 0.0 copy-done.1
  311.6 0.1 dynamic_slice.15
  311.7 0.0 copy-done.2
  311.7 0.1 dynamic_slice.14
  311.8 0.0 copy-done
  311.8 0.1 constant_dynamic-slice_fusion
  311.8 0.0 copy-done.3
  311.8 0.2 select_reduce_fusion
  312.1 0.2 select_reduce_fusion.2
  312.3 0.1 broadcast_xor_fusion
  312.4 0.2 broadcast_add_fusion
  312.6 24.4 %all-to-all-done = f32[2,128,1024]{1,0,2:T(2,128)S(1)} async-done(((f32[2,128,1024]{1,0,2:T(2,128)}), f32[2,128,1024]{1,0,2:T(2,128)S(1)}, u32[]{:S(2)}, u32[]{:S(2)}) %all-to-all-start) | async-done | bytes 1048608 | tf_op jit(solution)/shard_map/all_to_all | solution.py:33
  337.0 0.5 copy.16
  337.6 1.6 fusion.9
  339.2 1.3 copy.17
  (8 shorter events, 0.0 us)
Async XLA Ops:
  6.5 305.2 %copy-start = (s32[8,2]{0,1:T(2,128)S(1)}, s32[8,2]{0,1:T(2,128)}, u32[]{:S(2)}) copy-start(s32[8,2]{0,1:T(2,128)} %param.15) | copy-start | bytes 196
  6.5 79.1 %all-gather.2.cloned.1.call-start = ((), (), s32[]{:S(2)}) async-start(), calls=%async_computation.2 | async-start | bytes 4718592 | tf_op jit(solution)/shard_map/all_gather | solution.py:18
  7.3 273.6 %reduce-scatter.2.cloned.1.call-start = ((), (), s32[]{:S(2)}) async-start(), calls=%async_computation.3 | async-start | bytes 9437184 | tf_op jit(solution)/shard_map/reduce_scatter | solution.py:25
  133.0 178.6 %copy-start.1 = (f32[1024]{0:T(1024)S(1)}, f32[1024]{0:T(1024)}, u32[]{:S(2)}) copy-start(f32[1024]{0:T(1024)} %param.12) | copy-start | bytes 12292
  133.0 178.7 %copy-start.2 = (s32[1024]{0:T(1024)S(1)}, s32[1024]{0:T(1024)}, u32[]{:S(2)}) copy-start(s32[1024]{0:T(1024)} %param.14) | copy-start | bytes 12292
  133.0 178.8 %copy-start.3 = (f32[100]{0:T(128)S(1)}, f32[100]{0:T(128)}, u32[]{:S(2)}) copy-start(f32[100]{0:T(128)} %param.11) | copy-start | bytes 1204
  133.0 179.1 %copy-start.4 = (s32[100]{0:T(128)S(1)}, s32[100]{0:T(128)}, u32[]{:S(2)}) copy-start(s32[100]{0:T(128)} %param.13) | copy-start | bytes 1204
  280.9 25.2 %collective-permute-start = (f32[2,128,1024]{1,2,0:T(8,128)}, f32[2,128,1024]{1,2,0:T(8,128)S(1)}, u32[]{:S(2)}, u32[]{:S(2)}) collective-permute-start(f32[2,128,1024]{1,2,0:T(8,128)} %bitcast.45), channel_id=1, source_target_pairs={{16,0},{24,8},{0,16},{8,24},{17,1},{25,9},{1,17},{9,25},{18,2},{26... | collective-permute-start | bytes 3145736 | tf_op jit(solution)/shard_map/ppermute | solution.py:10
  307.8 29.2 %all-to-all-start = ((f32[2,128,1024]{1,0,2:T(2,128)}), f32[2,128,1024]{1,0,2:T(2,128)S(1)}, u32[]{:S(2)}, u32[]{:S(2)}) async-start(f32[2,128,1024]{1,0,2:T(2,128)} %copy.15), calls=%async_computation.1 | async-start | bytes 2097152 | tf_op jit(solution)/shard_map/all_to_all | solution.py:33
Sparse Core Ops, SparseCore 0:
  9.5 76.0 all-gather.1
  133.2 147.6 reduce-scatter.1
where the time goes:
time: 348 us; the launch traced here: 347 us
  waiting for transfers between devices  275 us (79%)
  matrix products  47.3 us (14%)
  between operations  13.5 us (4%)
  starting transfers between devices  5.3 us (2%)
  local copies, waits for them, and re-layouts  3.85 us (1%)
    reduce_scatter x1, waiting for transfers between devices, per_device(): lax.psum_scatter(jnp.einsum('qac,qpbc->apb', factors, halves, preferred_e...  148 us
    all_gather x1, waiting for transfers between devices, per_device(): gathered = lax.all_gather(amplitudes, 'vir', axis=1, tiled=True)  78.3 us
    dot_general x3, matrix products, half_product(): jnp.einsum('pcd,bd->pbc', gathered, factor, preferred_element_type=jnp.fl...  27.9 us
    all_to_all x1, waiting for transfers between devices, per_device(): lax.all_to_all(shifted, 'vir', split_axis=2, concat_axis=1, tiled=True)  24.4 us
    ppermute x1, waiting for transfers between devices, passed_along(): return lax.ppermute(block, axis, route)  23.7 us
    dot_general x1, matrix products, per_device(): jnp.einsum('qac,qpbc->apb', factors, halves, preferred_element_type=jnp.f...  19.4 us
  transfers between devices with their start and end apart: 4, of which 4 were waited for; matrix products, arithmetic and copies ran while one was open for 0% of the time, Pallas kernels for 0%

commit v1 on v0

v1 whole, which is shorter than its diff:
```python
import functools

import jax
import jax.numpy as jnp
from jax import lax
from jax.experimental import pallas as pl
from jax.experimental.pallas import tpu as pltpu
from jax.sharding import PartitionSpec as P

GROUP_ROWS = 256
ROW_CHUNK = 256


def dot_nt(left, right):
    return lax.dot_general(left, right, (((1,), (1,)), ((), ())), preferred_element_type=jnp.float32)


def ladder_kernel(kept_count, swapped_count, factor_count, has_total, place_ref, factor_ref, *refs):
    block_count = kept_count + swapped_count
    pair_refs = refs[: 2 * block_count]
    rest = refs[2 * block_count :]
    total_ref = rest[0] if has_total else None
    out_ref, rows_ref, left_ref, right_ref = rest[1:] if has_total else rest
    step = pl.program_id(0)
    size = factor_ref.shape[1]
    half = pair_refs[0].shape[0]
    width = block_count * GROUP_ROWS

    @pl.when(step == 0)
    def _():
        flip = place_ref[0]
        for block in range(block_count):
            first = block * GROUP_ROWS + flip * half
            second = block * GROUP_ROWS + (1 - flip) * half
            rows_ref[pl.ds(pl.multiple_of(first, half), half), :] = pair_refs[2 * block][...]
            rows_ref[pl.ds(pl.multiple_of(second, half), half), :] = pair_refs[2 * block + 1][...]

    for number in range(factor_count):

        @pl.when(step == number)
        def _():
            for chunk in range(size // ROW_CHUNK):
                here = pl.ds(chunk * ROW_CHUNK, ROW_CHUNK)
                halves = dot_nt(factor_ref[0, here, :], rows_ref[...]).astype(jnp.bfloat16)
                for block in range(block_count):
                    column = pl.multiple_of(place_ref[1 + block] * GROUP_ROWS, GROUP_ROWS)
                    taken = factor_ref[0, here, pl.ds(column, GROUP_ROWS)]
                    made = halves[:, block * GROUP_ROWS : (block + 1) * GROUP_ROWS]
                    target = pl.ds(number * width + block * GROUP_ROWS, GROUP_ROWS)
                    left_ref[here, target] = taken if block < kept_count else made
                    right_ref[here, target] = made if block < kept_count else taken

    @pl.when(step >= factor_count)
    def _():
        first = pl.multiple_of((step - factor_count) * ROW_CHUNK, ROW_CHUNK)
        product = dot_nt(left_ref[pl.ds(first, ROW_CHUNK), :], right_ref[...])
        out_ref[...] = product + total_ref[...] if has_total else product


def ladder(place, factors, kept, swapped, total):
    factor_count, size, _ = factors.shape
    pairs = list(kept) + list(swapped)
    width = len(pairs) * GROUP_ROWS
    chunk_count = size // ROW_CHUNK

    def factor_map(step, place_ref):
        return (jnp.minimum(step, factor_count - 1), 0, 0)

    def chunk_map(step, place_ref):
        return (jnp.maximum(step - factor_count, 0), 0)

    def whole_map(step, place_ref):
        return (0, 0)

    operands = [factors] + [half for pair in pairs for half in pair]
    in_specs = [pl.BlockSpec((1, size, size), factor_map)]
    in_specs += [pl.BlockSpec(half.shape, whole_map) for half in operands[1:]]
    if total is not None:
        operands.append(total)
        in_specs.append(pl.BlockSpec((ROW_CHUNK, size), chunk_map))
    return pl.pallas_call(
        functools.partial(ladder_kernel, len(kept), len(swapped), factor_count, total is not None),
        out_shape=jax.ShapeDtypeStruct((size, size), jnp.float32),
        grid_spec=pltpu.PrefetchScalarGridSpec(
            num_scalar_prefetch=1,
            grid=(factor_count + chunk_count,),
            in_specs=in_specs,
            out_specs=pl.BlockSpec((ROW_CHUNK, size), chunk_map),
            scratch_shapes=[
                pltpu.VMEM((width, size), jnp.bfloat16),
                pltpu.VMEM((size, factor_count * width), jnp.bfloat16),
                pltpu.VMEM((size, factor_count * width), jnp.bfloat16),
            ],
        ),
        compiler_params=pltpu.CompilerParams(vmem_limit_bytes=40 * 1024 * 1024),
        cost_estimate=pl.CostEstimate(
            flops=4 * factor_count * width * size * size,
            bytes_accessed=2 * factor_count * size * size + 8 * size * size + 2 * width * size,
            transcendentals=0,
        ),
    )(place, *operands)


def per_device(amplitudes, factors, occ_energy, vir_energy, occ_irrep, vir_irrep, pair_orbitals):
    local_pairs, row_count, size = amplitudes.shape
    occ_total = occ_energy.shape[0]
    occ_devices = lax.axis_size("occ")
    vir_devices = lax.axis_size("vir")
    inner = GROUP_ROWS // row_count
    outer = vir_devices // inner
    assert local_pairs == 2 and outer == 4 and inner * row_count == GROUP_ROWS
    occ_index = lax.axis_index("occ")
    vir_index = lax.axis_index("vir")
    z_index = vir_index // inner
    x_index = vir_index % inner
    side = occ_index // (occ_devices // 2)
    across = occ_devices // 2

    def z_swap(block, distance):
        route = [(i, (i // inner ^ distance) * inner + i % inner) for i in range(vir_devices)]
        return lax.ppermute(block, "vir", route)

    def y_swap(block):
        return lax.ppermute(block, "occ", [(i, (i + across) % occ_devices) for i in range(occ_devices)])

    inner_groups = [[g * inner + i for i in range(inner)] for g in range(outer)]

    def x_swap(block):
        return lax.ppermute(block, "vir", [(i, i ^ 1) for i in range(vir_devices)])

    def x_gather(blocks):
        if inner == 2:
            joined = blocks[0] if len(blocks) == 1 else jnp.concatenate(blocks, axis=0)
            came = x_swap(joined)
            return [(b, came[i * row_count : (i + 1) * row_count]) for i, b in enumerate(blocks)]
        pairs = []
        for block in blocks:
            whole = lax.all_gather(block, "vir", axis_index_groups=inner_groups, axis=0, tiled=True)
            pairs.append((whole[: GROUP_ROWS // 2], whole[GROUP_ROWS // 2 :]))
        return pairs

    def x_scatter(sums):
        if inner == 2:
            sent = lax.dynamic_index_in_dim(sums, 1 - x_index, 1, keepdims=False).astype(jnp.bfloat16)
            own = lax.dynamic_index_in_dim(sums, x_index, 1, keepdims=False)
            return own + x_swap(sent).astype(jnp.float32)
        return lax.psum_scatter(sums, "vir", scatter_dimension=1, axis_index_groups=inner_groups)

    def z_scatter(sums, axis, distance, bit):
        sent = lax.dynamic_index_in_dim(sums, 1 - bit, axis, keepdims=False).astype(jnp.bfloat16)
        own = lax.dynamic_index_in_dim(sums, bit, axis, keepdims=False)
        return own + z_swap(sent, distance).astype(jnp.float32)

    z_high = z_index // 2
    z_low = z_index % 2

    kept_0 = lax.dynamic_index_in_dim(amplitudes, side, 0, keepdims=False)
    given = lax.dynamic_index_in_dim(amplitudes, 1 - side, 0, keepdims=False)
    swapped_0 = y_swap(given)
    kept_2 = z_swap(kept_0, 2)
    swapped_2 = z_swap(swapped_0, 2)
    kept_13 = z_swap(jnp.concatenate([kept_0, kept_2], axis=0), 1)
    swapped_13 = z_swap(jnp.concatenate([swapped_0, swapped_2], axis=0), 1)
    kept_1, kept_3 = kept_13[:row_count], kept_13[row_count:]
    swapped_1, swapped_3 = swapped_13[:row_count], swapped_13[row_count:]

    (kept_pair_0,) = x_gather([kept_0])
    (swapped_pair_0,) = x_gather([swapped_0])
    (kept_pair_2,) = x_gather([kept_2])
    (swapped_pair_2,) = x_gather([swapped_2])
    kept_pair_1, kept_pair_3 = x_gather([kept_1, kept_3])
    swapped_pair_1, swapped_pair_3 = x_gather([swapped_1, swapped_3])

    flip = x_index if inner == 2 else jnp.int32(0)

    def place(*zs):
        return jnp.stack([flip, *[z_index ^ d for d in zs]]).astype(jnp.int32)

    total = ladder(place(0, 0), factors, [kept_pair_0], [swapped_pair_0], None)
    total = ladder(place(2, 2), factors, [kept_pair_2], [swapped_pair_2], total)
    total = ladder(place(1, 3), factors, [kept_pair_1, kept_pair_3], [], total)
    total = ladder(place(1, 3), factors, [], [swapped_pair_1, swapped_pair_3], total)

    middle = size // 2
    left = total[:, :middle].reshape(4, inner, row_count, middle)
    left = x_scatter(left)
    left = z_scatter(left.reshape(2, 2, row_count, middle), 1, 1, z_low)
    right = total[:, middle:].reshape(2, 2, GROUP_ROWS, middle)
    right = z_scatter(right, 1, 1, z_low)
    right = x_scatter(right.reshape(2, inner, row_count, middle))
    own_rows = z_scatter(jnp.concatenate([left, right], axis=2), 0, 2, z_high)

    packed = own_rows.astype(jnp.bfloat16).reshape(row_count, vir_devices, row_count)
    packed = jnp.transpose(packed, (1, 2, 0))
    if vir_devices == 8:
        def flipped(blocks):
            blocks = blocks.reshape(2, 2, 2, row_count, row_count)
            for axis in range(3):
                bit = (vir_index >> (2 - axis)) & 1
                blocks = jnp.where(bit == 1, jnp.flip(blocks, axis), blocks)
            return blocks.reshape(8, row_count, row_count)

        turned = flipped(packed)
        came = []
        for step in range(vir_devices):
            route = [
                (o * vir_devices + i, ((o + across) % occ_devices) * vir_devices + (i ^ step))
                for o in range(occ_devices)
                for i in range(vir_devices)
            ]
            came.append(lax.ppermute(turned[step], ("occ", "vir"), route))
        partner = flipped(jnp.stack(came))
    else:
        partner = y_swap(lax.all_to_all(packed, "vir", 0, 0))
    partner = jnp.transpose(partner, (1, 0, 2)).reshape(row_count, size).astype(jnp.float32)

    first = jnp.where(side == 0, own_rows, partner)
    second = jnp.where(side == 0, partner, own_rows)
    numerator = jnp.stack([first, second])

    pair_ids = lax.dynamic_slice_in_dim(pair_orbitals, occ_index * local_pairs, local_pairs, 0)
    row_start = vir_index * row_count
    energy_rows = lax.dynamic_slice_in_dim(vir_energy, row_start, row_count, 0)
    irrep_rows = lax.dynamic_slice_in_dim(vir_irrep, row_start, row_count, 0)
    positions = jnp.arange(occ_total, dtype=jnp.int32)
    first_hot = positions[None, :] == pair_ids[:, 0:1]
    second_hot = positions[None, :] == pair_ids[:, 1:2]
    pair_energy = jnp.sum(jnp.where(first_hot, occ_energy[None, :], 0.0), axis=1) + jnp.sum(
        jnp.where(second_hot, occ_energy[None, :], 0.0), axis=1
    )
    first_irrep = jnp.sum(jnp.where(first_hot, occ_irrep[None, :], 0), axis=1)
    second_irrep = jnp.sum(jnp.where(second_hot, occ_irrep[None, :], 0), axis=1)
    pair_sym = jnp.bitwise_xor(first_irrep, second_irrep)
    combined = jnp.bitwise_xor(
        jnp.bitwise_xor(pair_sym[:, None, None], irrep_rows[None, :, None]),
        vir_irrep[None, None, :],
    )
    allowed = combined == 0
    denominator = (
        energy_rows[None, :, None] + vir_energy[None, None, :] - pair_energy[:, None, None]
    )
    return jnp.where(allowed, numerator / denominator, jnp.float32(0.0))


def solution(mesh):
    return jax.shard_map(
        per_device,
        mesh=mesh,
        in_specs=(P("occ", "vir", None), P("vir", None, None), P(), P(), P(), P(), P()),
        out_specs=P("occ", "vir", None),
        check_vma=False,
    )
```

time: 348 us -> 142 us (0.41)
  waiting for transfers between devices: 275 us -> 48.6 us
  matrix products: 47.3 us -> 0 us
  Pallas kernels: 0 us -> 41 us
  starting transfers between devices: 5.3 us -> 37.4 us
  between operations: 13.5 us -> 0.41 us
  local copies, waits for them, and re-layouts: 3.85 us -> 8.76 us
    reduce_scatter x1 -> x0, waiting for transfers between devices: 148 us -> none  [per_device(): lax.psum_scatter(jnp.einsum('qac,qpbc->apb', factors, halves, preferred_e...]
    all_gather x1 -> x0, waiting for transfers between devices: 78.3 us -> none  [per_device(): gathered = lax.all_gather(amplitudes, 'vir', axis=1, tiled=True)]
    dot_general x4 -> x0, matrix products: 47.3 us -> none  [the longest x3 27.9 us: half_product(): jnp.einsum('pcd,bd->pbc', gathered, factor, preferred_element_type=jnp.fl...]
    pallas_call x0 -> x4, Pallas kernels: none -> 41 us  [ladder(): pl.pallas_call(functools.partial(ladder_kernel, len(kept), len(swapped),...]
    ppermute x1 -> x24, starting transfers between devices: 1.47 us -> 37.4 us  [the longest x8 15.5 us: per_device(): came.append(lax.ppermute(turned[step], ('occ', 'vir'), route))]
    ppermute x1 -> x24, waiting for transfers between devices: 23.7 us -> 48.6 us  [the longest x7 27.6 us: z_swap(): return lax.ppermute(block, 'vir', route)]
    all_to_all x1 -> x0, waiting for transfers between devices: 24.4 us -> none  [per_device(): lax.all_to_all(shifted, 'vir', split_axis=2, concat_axis=1, tiled=True)]
    unnamed x10 -> x24, local copies, waits for them, and re-layouts: 0.02 us -> 5.24 us
  transfers between devices with their start and end apart: 4 -> 24, of which waited for: 4 -> 11; matrix products, arithmetic and copies ran while one was open for 0% -> 3% of each run, Pallas kernels for 0% -> 21%
where the time goes in v1:
time: 142 us
  waiting for transfers between devices  48.6 us (34%)
  Pallas kernels  41 us (29%)
  starting transfers between devices  37.4 us (26%)
  local copies, waits for them, and re-layouts  8.76 us (6%)
  other arithmetic  5.69 us (4%)
    pallas_call x4, Pallas kernels, ladder(): pl.pallas_call(functools.partial(ladder_kernel, len(kept), len(swapped),...  41 us
    ppermute x7, waiting for transfers between devices, z_swap(): return lax.ppermute(block, 'vir', route)  27.6 us
    ppermute x8, starting transfers between devices, per_device(): came.append(lax.ppermute(turned[step], ('occ', 'vir'), route))  15.5 us
    ppermute x8, waiting for transfers between devices, x_swap(): return lax.ppermute(block, 'vir', [(i, i ^ 1) for i in range(vir_devices)])  13.2 us
    ppermute x7, starting transfers between devices, z_swap(): return lax.ppermute(block, 'vir', route)  10.8 us
    ppermute x8, starting transfers between devices, x_swap(): return lax.ppermute(block, 'vir', [(i, i ^ 1) for i in range(vir_devices)])  8.06 us
    ppermute x8, waiting for transfers between devices, per_device(): came.append(lax.ppermute(turned[step], ('occ', 'vir'), route))  5.65 us
    unnamed x24, local copies, waits for them, and re-layouts  5.24 us
  transfers between devices with their start and end apart: 24, of which 11 were waited for; matrix products, arithmetic and copies ran while one was open for 3% of the time, Pallas kernels for 21%

profile of v1, /device:TPU:0, one launch (start us, length us, event | category | flops | bytes accessed | tf_op | source)
XLA Modules:
  0.0 141.9 jit_solution(12525924281885184297)
XLA Ops:
  0.0 1.1 dynamic-slice_bitcast_fusion
  1.1 3.0 %collective-permute-start = (bf16[128,1024]{1,0:T(8,128)(2,1)S(1)}, bf16[128,1024]{1,0:T(8,128)(2,1)S(1)}, u32[]{:S(2)}, u32[]{:S(2)}) collective-permute-start(bf16[128,1024]{1,0:T(8,128)(2,1)S(1)} %get-tuple-element.20), channel_id=1, source_target_pairs={{0,16},{8,24},{16,0},{24,8},{1,17},{9,25},{17,1},{25,9},{2,18},{10... | collective-permute-start | bytes 786440 | tf_op jit(solution)/shard_map/ppermute | solution.py:124
  4.1 1.5 %collective-permute-start.9 = (bf16[128,1024]{1,0:T(8,128)(2,1)S(1)}, bf16[128,1024]{1,0:T(8,128)(2,1)S(1)}, u32[]{:S(2)}, u32[]{:S(2)}) collective-permute-start(bf16[128,1024]{1,0:T(8,128)(2,1)S(1)} %get-tuple-element.19.refs_0_), channel_id=1, source_target_pairs={{0,1},{1,0},{2,3},{3,2},{4,5},{5,4},{6,7},{7,6},{8,9},{9,8},{10,11... | collective-permute-start | bytes 786440 | tf_op jit(solution)/shard_map/ppermute | solution.py:129
  5.6 2.6 %collective-permute-start.4 = (bf16[128,1024]{1,0:T(8,128)(2,1)S(1)}, bf16[128,1024]{1,0:T(8,128)(2,1)S(1)}, u32[]{:S(2)}, u32[]{:S(2)}) collective-permute-start(bf16[128,1024]{1,0:T(8,128)(2,1)S(1)} %get-tuple-element.19.refs_0_), channel_id=1, source_target_pairs={{0,4},{1,5},{2,6},{3,7},{4,0},{5,1},{6,2},{7,3},{8,12},{9,13},{10,... | collective-permute-start | bytes 786440 | tf_op jit(solution)/shard_map/ppermute | solution.py:121
  8.3 2.1 %collective-permute-done.refs_2_ = bf16[128,1024]{1,0:T(8,128)(2,1)S(1)} collective-permute-done((bf16[128,1024]{1,0:T(8,128)(2,1)S(1)}, bf16[128,1024]{1,0:T(8,128)(2,1)S(1)}, u32[]{:S(2)}, u32[]{:S(2)}) %collective-permute-start) | collective-permute-done | bytes 262176 | tf_op jit(solution)/shard_map/ppermute | solution.py:124
  10.4 2.8 %collective-permute-start.1 = (bf16[128,1024]{1,0:T(8,128)(2,1)S(1)}, bf16[128,1024]{1,0:T(8,128)(2,1)S(1)}, u32[]{:S(2)}, u32[]{:S(2)}) collective-permute-start(bf16[128,1024]{1,0:T(8,128)(2,1)S(1)} %collective-permute-done.refs_2_), channel_id=1, source_target_pairs={{0,4},{1,5},{2,6},{3,7},{4,0},{5,1},{6,2},{7,3},{8,12},{9,13},{10,... | collective-permute-start | bytes 786440 | tf_op jit(solution)/shard_map/ppermute | solution.py:121
  13.3 1.5 %collective-permute-start.10 = (bf16[128,1024]{1,0:T(8,128)(2,1)S(1)}, bf16[128,1024]{1,0:T(8,128)(2,1)S(1)}, u32[]{:S(2)}, u32[]{:S(2)}) collective-permute-start(bf16[128,1024]{1,0:T(8,128)(2,1)S(1)} %collective-permute-done.refs_2_), channel_id=1, source_target_pairs={{0,1},{1,0},{2,3},{3,2},{4,5},{5,4},{6,7},{7,6},{8,9},{9,8},{10,11... | collective-permute-start | bytes 786440 | tf_op jit(solution)/shard_map/ppermute | solution.py:129
  14.9 11.5 %collective-permute-done.4.refs_0_ = bf16[128,1024]{1,0:T(8,128)(2,1)S(1)} collective-permute-done((bf16[128,1024]{1,0:T(8,128)(2,1)S(1)}, bf16[128,1024]{1,0:T(8,128)(2,1)S(1)}, u32[]{:S(2)}, u32[]{:S(2)}) %collective-permute-start.4) | collective-permute-done | bytes 262176 | tf_op jit(solution)/shard_map/ppermute | solution.py:121
  27.1 3.8 %collective-permute-done.1.refs_2_ = bf16[128,1024]{1,0:T(8,128)(2,1)S(1)} collective-permute-done((bf16[128,1024]{1,0:T(8,128)(2,1)S(1)}, bf16[128,1024]{1,0:T(8,128)(2,1)S(1)}, u32[]{:S(2)}, u32[]{:S(2)}) %collective-permute-start.1) | collective-permute-done | bytes 262176 | tf_op jit(solution)/shard_map/ppermute | solution.py:121
  32.2 2.8 %copy-done.1 = bf16[3,1024,1024]{2,1,0:T(8,128)(2,1)S(1)} copy-done((bf16[3,1024,1024]{2,1,0:T(8,128)(2,1)S(1)}, bf16[3,1024,1024]{2,1,0:T(8,128)(2,1)}, u32[]{:S(2)}) %copy-start.1) | copy-done | bytes 6291480
  35.0 8.7 %shard_map.73.refs_4_ = f32[1024,1024]{1,0:T(8,128)S(1)} custom-call(s32[3]{0:T(128)S(1)} %pad_add_fusion.2.place_ref, bf16[3,1024,1024]{2,1,0:T(8,128)(2,1)S(1)} %copy-done.1, bf16[128,1024]{1,0:T(8,128)(2,1)S(1)} %get-tuple-element.19.refs_0_, bf16[128,1024]{1,0:T(8,128)(2,1)S(1)} %collective-permute-done.9.refs_1_, ...), custom_call_target="tpu_custom_call" | custom-call | flops 6442450944 | bytes 15728640 | tf_op jit(solution)/shard_map/pallas_call | solution.py:81
  43.7 1.6 %collective-permute-start.6 = (bf16[256,1024]{1,0:T(8,128)(2,1)S(1)}, bf16[256,1024]{1,0:T(8,128)(2,1)S(1)}, u32[]{:S(2)}, u32[]{:S(2)}) collective-permute-start(bf16[256,1024]{1,0:T(8,128)(2,1)S(1)} %collective-permute-done.5), channel_id=1, source_target_pairs={{0,1},{1,0},{2,3},{3,2},{4,5},{5,4},{6,7},{7,6},{8,9},{9,8},{10,11... | collective-permute-start | bytes 1572872 | tf_op jit(solution)/shard_map/ppermute | solution.py:129
  45.3 10.7 %shard_map.74.refs_4_ = f32[1024,1024]{1,0:T(8,128)S(1)} custom-call(s32[3]{0:T(128)S(1)} %pad_add_fusion.1.place_ref, bf16[3,1024,1024]{2,1,0:T(8,128)(2,1)} %factor_ref.7, bf16[128,1024]{1,0:T(8,128)(2,1)S(1)} %collective-permute-done.4.refs_0_, bf16[128,1024]{1,0:T(8,128)(2,1)S(1)} %collective-permute-done.7.refs_1_, ...), custom_call_target="tpu_custom_call" | custom-call | flops 6442450944 | bytes 15728640 | tf_op jit(solution)/shard_map/pallas_call | solution.py:81
  57.1 10.8 %shard_map.75.refs_4_ = f32[1024,1024]{1,0:T(8,128)S(1)} custom-call(s32[3]{0:T(128)S(1)} %pad_add_fusion.place_ref, bf16[3,1024,1024]{2,1,0:T(8,128)(2,1)} %factor_ref.7, bf16[128,1024]{1,0:T(8,128)(2,1)S(1)} %get-tuple-element.18.refs_0_, bf16[128,1024]{1,0:T(8,128)(2,1)S(1)} %get-tuple-element.16.refs_1_, ...), custom_call_target="tpu_custom_call" | custom-call | flops 6442450944 | bytes 15728640 | tf_op jit(solution)/shard_map/pallas_call | solution.py:81
  67.9 1.2 collective-permute-done.3
  69.1 10.8 %shard_map.76 = f32[1024,1024]{1,0:T(8,128)S(1)} custom-call(s32[3]{0:T(128)S(1)} %pad_add_fusion.place_ref, bf16[3,1024,1024]{2,1,0:T(8,128)(2,1)} %factor_ref.7, bf16[128,1024]{1,0:T(8,128)(2,1)S(1)} %get-tuple-element.24.refs_0_, bf16[128,1024]{1,0:T(8,128)(2,1)S(1)} %get-tuple-element.22.refs_1_, bf16[128,1024]{1,0:T(8,128)(2,1)S(1)} %get-tuple-element.23.refs_2_, ...), custom_call_target="tpu_custom_call" | custom-call | flops 6442450944 | bytes 15728640 | tf_op jit(solution)/shard_map/pallas_call | solution.py:81
  80.5 1.4 copy-done.2
  83.5 10.6 %collective-permute-done.11 = bf16[4,128,512]{2,1,0:T(8,128)(2,1)} collective-permute-done((bf16[4,128,512]{2,1,0:T(8,128)(2,1)S(1)}, bf16[4,128,512]{2,1,0:T(8,128)(2,1)}, u32[]{:S(2)}, u32[]{:S(2)}) %collective-permute-start.11) | collective-permute-done | bytes 524320 | tf_op jit(solution)/shard_map/ppermute | solution.py:129
  94.2 1.6 %bitcast_add_fusion.1 = f32[4,128,512]{2,1,0:T(8,128)S(1)} fusion(bf16[4,128,512]{2,1,0:T(8,128)(2,1)} %collective-permute-done.11, f32[4,2,128,512]{3,2,1,0:T(8,128)} %bitcast.111, s32[]{:T(128)S(6)} %select_n.133), kind=kLoop, calls=%fused_computation.9 | loop fusion | flops 524288 | bytes 2621444 | tf_op jit(solution)/shard_map/add | solution.py:146
  99.1 4.0 %collective-permute-done.12 = bf16[2,128,512]{2,1,0:T(8,128)(2,1)S(1)} collective-permute-done((bf16[2,128,512]{2,1,0:T(8,128)(2,1)}, bf16[2,128,512]{2,1,0:T(8,128)(2,1)S(1)}, u32[]{:S(2)}, u32[]{:S(2)}) %collective-permute-start.12) | collective-permute-done | bytes 262176 | tf_op jit(solution)/shard_map/ppermute | solution.py:121
  104.2 1.1 bitcast_add_fusion.2
  105.3 4.0 %collective-permute-start.15 = (bf16[128,1024]{1,0:T(8,128)(2,1)S(1)}, bf16[128,1024]{1,0:T(8,128)(2,1)S(1)}, u32[]{:S(2)}, u32[]{:S(2)}) collective-permute-start(bf16[128,1024]{1,0:T(8,128)(2,1)S(1)} %fusion.13), channel_id=1, source_target_pairs={{0,4},{1,5},{2,6},{3,7},{4,0},{5,1},{6,2},{7,3},{8,12},{9,13},{10,... | collective-permute-start | bytes 786440 | tf_op jit(solution)/shard_map/ppermute | solution.py:121
  109.6 8.2 %collective-permute-done.15 = bf16[128,1024]{1,0:T(8,128)(2,1)S(1)} collective-permute-done((bf16[128,1024]{1,0:T(8,128)(2,1)S(1)}, bf16[128,1024]{1,0:T(8,128)(2,1)S(1)}, u32[]{:S(2)}, u32[]{:S(2)}) %collective-permute-start.15) | collective-permute-done | bytes 262176 | tf_op jit(solution)/shard_map/ppermute | solution.py:121
  119.2 2.3 %collective-permute-start.17 = (bf16[128,128]{1,0:T(8,128)(2,1)S(1)}, bf16[128,128]{1,0:T(8,128)(2,1)S(1)}, u32[]{:S(2)}, u32[]{:S(2)}) collective-permute-start(bf16[128,128]{1,0:T(8,128)(2,1)S(1)} %get-tuple-element.31), channel_id=1, source_target_pairs={{0,17},{1,16},{2,19},{3,18},{4,21},{5,20},{6,23},{7,22},{8,25},{9,... | collective-permute-start | bytes 98312 | tf_op jit(solution)/shard_map/ppermute | solution.py:211
  121.8 2.8 %collective-permute-start.19 = (bf16[128,128]{1,0:T(8,128)(2,1)S(1)}, bf16[128,128]{1,0:T(8,128)(2,1)S(1)}, u32[]{:S(2)}, u32[]{:S(2)}) collective-permute-start(bf16[128,128]{1,0:T(8,128)(2,1)S(1)} %get-tuple-element.29), channel_id=1, source_target_pairs={{0,19},{1,18},{2,17},{3,16},{4,23},{5,22},{6,21},{7,20},{8,27},{9,... | collective-permute-start | bytes 98312 | tf_op jit(solution)/shard_map/ppermute | solution.py:211
  124.6 1.8 %collective-permute-start.20 = (bf16[128,128]{1,0:T(8,128)(2,1)S(1)}, bf16[128,128]{1,0:T(8,128)(2,1)S(1)}, u32[]{:S(2)}, u32[]{:S(2)}) collective-permute-start(bf16[128,128]{1,0:T(8,128)(2,1)S(1)} %get-tuple-element.28), channel_id=1, source_target_pairs={{0,20},{1,21},{2,22},{3,23},{4,16},{5,17},{6,18},{7,19},{8,28},{9,... | collective-permute-start | bytes 98312 | tf_op jit(solution)/shard_map/ppermute | solution.py:211
  126.4 2.8 %collective-permute-start.21 = (bf16[128,128]{1,0:T(8,128)(2,1)S(1)}, bf16[128,128]{1,0:T(8,128)(2,1)S(1)}, u32[]{:S(2)}, u32[]{:S(2)}) collective-permute-start(bf16[128,128]{1,0:T(8,128)(2,1)S(1)} %get-tuple-element.27), channel_id=1, source_target_pairs={{0,21},{1,20},{2,23},{3,22},{4,17},{5,16},{6,19},{7,18},{8,29},{9,... | collective-permute-start | bytes 98312 | tf_op jit(solution)/shard_map/ppermute | solution.py:211
  129.2 3.1 %collective-permute-start.22 = (bf16[128,128]{1,0:T(8,128)(2,1)S(1)}, bf16[128,128]{1,0:T(8,128)(2,1)S(1)}, u32[]{:S(2)}, u32[]{:S(2)}) collective-permute-start(bf16[128,128]{1,0:T(8,128)(2,1)S(1)} %get-tuple-element.26), channel_id=1, source_target_pairs={{0,22},{1,23},{2,20},{3,21},{4,18},{5,19},{6,16},{7,17},{8,30},{9,... | collective-permute-start | bytes 98312 | tf_op jit(solution)/shard_map/ppermute | solution.py:211
  132.3 1.9 %collective-permute-start.23 = (bf16[128,128]{1,0:T(8,128)(2,1)S(1)}, bf16[128,128]{1,0:T(8,128)(2,1)S(1)}, u32[]{:S(2)}, u32[]{:S(2)}) collective-permute-start(bf16[128,128]{1,0:T(8,128)(2,1)S(1)} %get-tuple-element.25), channel_id=1, source_target_pairs={{0,23},{1,22},{2,21},{3,20},{4,19},{5,18},{6,17},{7,16},{8,31},{9,... | collective-permute-start | bytes 98312 | tf_op jit(solution)/shard_map/ppermute | solution.py:211
  134.3 1.5 %collective-permute-done.22 = bf16[128,128]{1,0:T(8,128)(2,1)S(1)} collective-permute-done((bf16[128,128]{1,0:T(8,128)(2,1)S(1)}, bf16[128,128]{1,0:T(8,128)(2,1)S(1)}, u32[]{:S(2)}, u32[]{:S(2)}) %collective-permute-start.22) | collective-permute-done | bytes 32800 | tf_op jit(solution)/shard_map/ppermute | solution.py:211
  135.8 4.1 %collective-permute-done.23 = bf16[128,128]{1,0:T(8,128)(2,1)S(1)} collective-permute-done((bf16[128,128]{1,0:T(8,128)(2,1)S(1)}, bf16[128,128]{1,0:T(8,128)(2,1)S(1)}, u32[]{:S(2)}, u32[]{:S(2)}) %collective-permute-start.23) | collective-permute-done | bytes 32800 | tf_op jit(solution)/shard_map/ppermute | solution.py:211
  140.7 1.2 fusion
  (87 shorter events, 12.6 us)
Async XLA Ops:
  0.0 82.7 %copy-start = (s32[8,2]{0,1:T(2,128)S(1)}, s32[8,2]{0,1:T(2,128)}, u32[]{:S(2)}) copy-start(s32[8,2]{0,1:T(2,128)} %param.13) | copy-start | bytes 196
  1.1 9.3 %collective-permute-start = (bf16[128,1024]{1,0:T(8,128)(2,1)S(1)}, bf16[128,1024]{1,0:T(8,128)(2,1)S(1)}, u32[]{:S(2)}, u32[]{:S(2)}) collective-permute-start(bf16[128,1024]{1,0:T(8,128)(2,1)S(1)} %get-tuple-element.20), channel_id=1, source_target_pairs={{0,16},{8,24},{16,0},{24,8},{1,17},{9,25},{17,1},{25,9},{2,18},{10... | collective-permute-start | bytes 786440 | tf_op jit(solution)/shard_map/ppermute | solution.py:124
  4.1 27.6 %collective-permute-start.9 = (bf16[128,1024]{1,0:T(8,128)(2,1)S(1)}, bf16[128,1024]{1,0:T(8,128)(2,1)S(1)}, u32[]{:S(2)}, u32[]{:S(2)}) collective-permute-start(bf16[128,1024]{1,0:T(8,128)(2,1)S(1)} %get-tuple-element.19.refs_0_), channel_id=1, source_target_pairs={{0,1},{1,0},{2,3},{3,2},{4,5},{5,4},{6,7},{7,6},{8,9},{9,8},{10,11... | collective-permute-start | bytes 786440 | tf_op jit(solution)/shard_map/ppermute | solution.py:129
  5.6 20.8 %collective-permute-start.4 = (bf16[128,1024]{1,0:T(8,128)(2,1)S(1)}, bf16[128,1024]{1,0:T(8,128)(2,1)S(1)}, u32[]{:S(2)}, u32[]{:S(2)}) collective-permute-start(bf16[128,1024]{1,0:T(8,128)(2,1)S(1)} %get-tuple-element.19.refs_0_), channel_id=1, source_target_pairs={{0,4},{1,5},{2,6},{3,7},{4,0},{5,1},{6,2},{7,3},{8,12},{9,13},{10,... | collective-permute-start | bytes 786440 | tf_op jit(solution)/shard_map/ppermute | solution.py:121
  10.4 20.5 %collective-permute-start.1 = (bf16[128,1024]{1,0:T(8,128)(2,1)S(1)}, bf16[128,1024]{1,0:T(8,128)(2,1)S(1)}, u32[]{:S(2)}, u32[]{:S(2)}) collective-permute-start(bf16[128,1024]{1,0:T(8,128)(2,1)S(1)} %collective-permute-done.refs_2_), channel_id=1, source_target_pairs={{0,4},{1,5},{2,6},{3,7},{4,0},{5,1},{6,2},{7,3},{8,12},{9,13},{10,... | collective-permute-start | bytes 786440 | tf_op jit(solution)/shard_map/ppermute | solution.py:121
  13.3 18.9 %collective-permute-start.10 = (bf16[128,1024]{1,0:T(8,128)(2,1)S(1)}, bf16[128,1024]{1,0:T(8,128)(2,1)S(1)}, u32[]{:S(2)}, u32[]{:S(2)}) collective-permute-start(bf16[128,1024]{1,0:T(8,128)(2,1)S(1)} %collective-permute-done.refs_2_), channel_id=1, source_target_pairs={{0,1},{1,0},{2,3},{3,2},{4,5},{5,4},{6,7},{7,6},{8,9},{9,8},{10,11... | collective-permute-start | bytes 786440 | tf_op jit(solution)/shard_map/ppermute | solution.py:129
  26.4 17.2 %collective-permute-start.5 = (bf16[256,1024]{1,0:T(8,128)(2,1)S(1)}, bf16[256,1024]{1,0:T(8,128)(2,1)S(1)}, u32[]{:S(2)}, u32[]{:S(2)}) collective-permute-start(bf16[256,1024]{1,0:T(8,128)(2,1)S(1)} %pad_maximum_fusion.1), channel_id=1, source_target_pairs={{0,2},{1,3},{2,0},{3,1},{4,6},{5,7},{6,4},{7,5},{8,10},{9,11},{10,... | collective-permute-start | bytes 1572872 | tf_op jit(solution)/shard_map/ppermute | solution.py:121
  26.5 18.7 %collective-permute-start.7 = (bf16[128,1024]{1,0:T(8,128)(2,1)S(1)}, bf16[128,1024]{1,0:T(8,128)(2,1)S(1)}, u32[]{:S(2)}, u32[]{:S(2)}) collective-permute-start(bf16[128,1024]{1,0:T(8,128)(2,1)S(1)} %collective-permute-done.4.refs_0_), channel_id=1, source_target_pairs={{0,1},{1,0},{2,3},{3,2},{4,5},{5,4},{6,7},{7,6},{8,9},{9,8},{10,11... | collective-permute-start | bytes 786440 | tf_op jit(solution)/shard_map/ppermute | solution.py:129
  31.0 25.0 %collective-permute-start.2 = (bf16[256,1024]{1,0:T(8,128)(2,1)S(1)}, bf16[256,1024]{1,0:T(8,128)(2,1)S(1)}, u32[]{:S(2)}, u32[]{:S(2)}) collective-permute-start(bf16[256,1024]{1,0:T(8,128)(2,1)S(1)} %pad_maximum_fusion), channel_id=1, source_target_pairs={{0,2},{1,3},{2,0},{3,1},{4,6},{5,7},{6,4},{7,5},{8,10},{9,11},{10,... | collective-permute-start | bytes 1572872 | tf_op jit(solution)/shard_map/ppermute | solution.py:121
  31.7 13.6 %collective-permute-start.8 = (bf16[128,1024]{1,0:T(8,128)(2,1)S(1)}, bf16[128,1024]{1,0:T(8,128)(2,1)S(1)}, u32[]{:S(2)}, u32[]{:S(2)}) collective-permute-start(bf16[128,1024]{1,0:T(8,128)(2,1)S(1)} %collective-permute-done.1.refs_2_), channel_id=1, source_target_pairs={{0,1},{1,0},{2,3},{3,2},{4,5},{5,4},{6,7},{7,6},{8,9},{9,8},{10,11... | collective-permute-start | bytes 786440 | tf_op jit(solution)/shard_map/ppermute | solution.py:129
  32.2 2.8 %copy-start.1 = (bf16[3,1024,1024]{2,1,0:T(8,128)(2,1)S(1)}, bf16[3,1024,1024]{2,1,0:T(8,128)(2,1)}, u32[]{:S(2)}) copy-start(bf16[3,1024,1024]{2,1,0:T(8,128)(2,1)} %factor_ref.7) | copy-start | bytes 18874372
  43.7 13.4 %collective-permute-start.6 = (bf16[256,1024]{1,0:T(8,128)(2,1)S(1)}, bf16[256,1024]{1,0:T(8,128)(2,1)S(1)}, u32[]{:S(2)}, u32[]{:S(2)}) collective-permute-start(bf16[256,1024]{1,0:T(8,128)(2,1)S(1)} %collective-permute-done.5), channel_id=1, source_target_pairs={{0,1},{1,0},{2,3},{3,2},{4,5},{5,4},{6,7},{7,6},{8,9},{9,8},{10,11... | collective-permute-start | bytes 1572872 | tf_op jit(solution)/shard_map/ppermute | solution.py:129
  56.0 13.1 %collective-permute-start.3 = (bf16[256,1024]{1,0:T(8,128)(2,1)S(1)}, bf16[256,1024]{1,0:T(8,128)(2,1)S(1)}, u32[]{:S(2)}, u32[]{:S(2)}) collective-permute-start(bf16[256,1024]{1,0:T(8,128)(2,1)S(1)} %collective-permute-done.2), channel_id=1, source_target_pairs={{0,1},{1,0},{2,3},{3,2},{4,5},{5,4},{6,7},{7,6},{8,9},{9,8},{10,11... | collective-permute-start | bytes 1572872 | tf_op jit(solution)/shard_map/ppermute | solution.py:129
  80.5 1.4 copy-start.2
  81.9 12.3 %collective-permute-start.11 = (bf16[4,128,512]{2,1,0:T(8,128)(2,1)S(1)}, bf16[4,128,512]{2,1,0:T(8,128)(2,1)}, u32[]{:S(2)}, u32[]{:S(2)}) collective-permute-start(bf16[4,128,512]{2,1,0:T(8,128)(2,1)S(1)} %fusion.2), channel_id=1, source_target_pairs={{0,1},{1,0},{2,3},{3,2},{4,5},{5,4},{6,7},{7,6},{8,9},{9,8},{10,11... | collective-permute-start | bytes 1572872 | tf_op jit(solution)/shard_map/ppermute | solution.py:129
  82.8 13.7 %collective-permute-start.13 = (bf16[2,256,512]{2,1,0:T(8,128)(2,1)S(1)}, bf16[2,256,512]{2,1,0:T(8,128)(2,1)S(1)}, u32[]{:S(2)}, u32[]{:S(2)}) collective-permute-start(bf16[2,256,512]{2,1,0:T(8,128)(2,1)S(1)} %fusion.1), channel_id=1, source_target_pairs={{0,2},{1,3},{2,0},{3,1},{4,6},{5,7},{6,4},{7,5},{8,10},{9,11},{10,... | collective-permute-start | bytes 1572872 | tf_op jit(solution)/shard_map/ppermute | solution.py:121
  95.8 3.0 %copy-start.6 = (s32[100]{0:T(128)S(1)}, s32[100]{0:T(128)}, u32[]{:S(2)}) copy-start(s32[100]{0:T(128)} %param.11) | copy-start | bytes 1204
  95.8 3.2 %copy-start.5 = (s32[1024]{0:T(1024)S(1)}, s32[1024]{0:T(1024)}, u32[]{:S(2)}) copy-start(s32[1024]{0:T(1024)} %param.12) | copy-start | bytes 12292
  96.5 6.6 %collective-permute-start.12 = (bf16[2,128,512]{2,1,0:T(8,128)(2,1)}, bf16[2,128,512]{2,1,0:T(8,128)(2,1)S(1)}, u32[]{:S(2)}, u32[]{:S(2)}) collective-permute-start(bf16[2,128,512]{2,1,0:T(8,128)(2,1)} %fusion.11), channel_id=1, source_target_pairs={{0,2},{1,3},{2,0},{3,1},{4,6},{5,7},{6,4},{7,5},{8,10},{9,11},{10,... | collective-permute-start | bytes 786440 | tf_op jit(solution)/shard_map/ppermute | solution.py:121
  96.7 1.0 copy-start.3
  97.7 11.7 %copy-start.4 = (f32[1024]{0:T(1024)S(1)}, f32[1024]{0:T(1024)}, u32[]{:S(2)}) copy-start(f32[1024]{0:T(1024)} %param.10) | copy-start | bytes 12292
  97.7 6.4 %collective-permute-start.14 = (bf16[2,128,512]{2,1,0:T(8,128)(2,1)S(1)}, bf16[2,128,512]{2,1,0:T(8,128)(2,1)S(1)}, u32[]{:S(2)}, u32[]{:S(2)}) collective-permute-start(bf16[2,128,512]{2,1,0:T(8,128)(2,1)S(1)} %fusion.12), channel_id=1, source_target_pairs={{0,1},{1,0},{2,3},{3,2},{4,5},{5,4},{6,7},{7,6},{8,9},{9,8},{10,11... | collective-permute-start | bytes 786440 | tf_op jit(solution)/shard_map/ppermute | solution.py:129
  105.3 12.5 %collective-permute-start.15 = (bf16[128,1024]{1,0:T(8,128)(2,1)S(1)}, bf16[128,1024]{1,0:T(8,128)(2,1)S(1)}, u32[]{:S(2)}, u32[]{:S(2)}) collective-permute-start(bf16[128,1024]{1,0:T(8,128)(2,1)S(1)} %fusion.13), channel_id=1, source_target_pairs={{0,4},{1,5},{2,6},{3,7},{4,0},{5,1},{6,2},{7,3},{8,12},{9,13},{10,... | collective-permute-start | bytes 786440 | tf_op jit(solution)/shard_map/ppermute | solution.py:121
  117.9 1.1 copy-start.7
  118.4 8.0 %collective-permute-start.16 = (bf16[128,128]{1,0:T(8,128)(2,1)S(1)}, bf16[128,128]{1,0:T(8,128)(2,1)S(1)}, u32[]{:S(2)}, u32[]{:S(2)}) collective-permute-start(bf16[128,128]{1,0:T(8,128)(2,1)S(1)} %get-tuple-element.32), channel_id=1, source_target_pairs={{0,16},{1,17},{2,18},{3,19},{4,20},{5,21},{6,22},{7,23},{8,24},{9,... | collective-permute-start | bytes 98312 | tf_op jit(solution)/shard_map/ppermute | solution.py:211
  119.2 9.9 %collective-permute-start.17 = (bf16[128,128]{1,0:T(8,128)(2,1)S(1)}, bf16[128,128]{1,0:T(8,128)(2,1)S(1)}, u32[]{:S(2)}, u32[]{:S(2)}) collective-permute-start(bf16[128,128]{1,0:T(8,128)(2,1)S(1)} %get-tuple-element.31), channel_id=1, source_target_pairs={{0,17},{1,16},{2,19},{3,18},{4,21},{5,20},{6,23},{7,22},{8,25},{9,... | collective-permute-start | bytes 98312 | tf_op jit(solution)/shard_map/ppermute | solution.py:211
  121.5 10.8 %collective-permute-start.18 = (bf16[128,128]{1,0:T(8,128)(2,1)S(1)}, bf16[128,128]{1,0:T(8,128)(2,1)S(1)}, u32[]{:S(2)}, u32[]{:S(2)}) collective-permute-start(bf16[128,128]{1,0:T(8,128)(2,1)S(1)} %get-tuple-element.30), channel_id=1, source_target_pairs={{0,18},{1,19},{2,16},{3,17},{4,22},{5,23},{6,20},{7,21},{8,26},{9,... | collective-permute-start | bytes 98312 | tf_op jit(solution)/shard_map/ppermute | solution.py:211
  121.8 12.4 %collective-permute-start.19 = (bf16[128,128]{1,0:T(8,128)(2,1)S(1)}, bf16[128,128]{1,0:T(8,128)(2,1)S(1)}, u32[]{:S(2)}, u32[]{:S(2)}) collective-permute-start(bf16[128,128]{1,0:T(8,128)(2,1)S(1)} %get-tuple-element.29), channel_id=1, source_target_pairs={{0,19},{1,18},{2,17},{3,16},{4,23},{5,22},{6,21},{7,20},{8,27},{9,... | collective-permute-start | bytes 98312 | tf_op jit(solution)/shard_map/ppermute | solution.py:211
  124.6 9.6 %collective-permute-start.20 = (bf16[128,128]{1,0:T(8,128)(2,1)S(1)}, bf16[128,128]{1,0:T(8,128)(2,1)S(1)}, u32[]{:S(2)}, u32[]{:S(2)}) collective-permute-start(bf16[128,128]{1,0:T(8,128)(2,1)S(1)} %get-tuple-element.28), channel_id=1, source_target_pairs={{0,20},{1,21},{2,22},{3,23},{4,16},{5,17},{6,18},{7,19},{8,28},{9,... | collective-permute-start | bytes 98312 | tf_op jit(solution)/shard_map/ppermute | solution.py:211
  126.4 7.8 %collective-permute-start.21 = (bf16[128,128]{1,0:T(8,128)(2,1)S(1)}, bf16[128,128]{1,0:T(8,128)(2,1)S(1)}, u32[]{:S(2)}, u32[]{:S(2)}) collective-permute-start(bf16[128,128]{1,0:T(8,128)(2,1)S(1)} %get-tuple-element.27), channel_id=1, source_target_pairs={{0,21},{1,20},{2,23},{3,22},{4,17},{5,16},{6,19},{7,18},{8,29},{9,... | collective-permute-start | bytes 98312 | tf_op jit(solution)/shard_map/ppermute | solution.py:211
  129.2 6.6 %collective-permute-start.22 = (bf16[128,128]{1,0:T(8,128)(2,1)S(1)}, bf16[128,128]{1,0:T(8,128)(2,1)S(1)}, u32[]{:S(2)}, u32[]{:S(2)}) collective-permute-start(bf16[128,128]{1,0:T(8,128)(2,1)S(1)} %get-tuple-element.26), channel_id=1, source_target_pairs={{0,22},{1,23},{2,20},{3,21},{4,18},{5,19},{6,16},{7,17},{8,30},{9,... | collective-permute-start | bytes 98312 | tf_op jit(solution)/shard_map/ppermute | solution.py:211
  132.3 7.6 %collective-permute-start.23 = (bf16[128,128]{1,0:T(8,128)(2,1)S(1)}, bf16[128,128]{1,0:T(8,128)(2,1)S(1)}, u32[]{:S(2)}, u32[]{:S(2)}) collective-permute-start(bf16[128,128]{1,0:T(8,128)(2,1)S(1)} %get-tuple-element.25), channel_id=1, source_target_pairs={{0,23},{1,22},{2,21},{3,20},{4,19},{5,18},{6,17},{7,16},{8,31},{9,... | collective-permute-start | bytes 98312 | tf_op jit(solution)/shard_map/ppermute | solution.py:211
